TPU v7x, 32 devices: a whole 2x2x4 slice. The times are simulated.
32 devices in a mesh: groups: 2 (over y), tm: 4 (over z), tile: 2 (over x), arrow: 2 (over core).
Axes of the slice: x: 2, y: 2, z: 4, core: 2. Of those that a mesh axis runs over, the one named last changes fastest.
Arguments:
- forward_blocks: float32 [8, 96, 1024], P(('groups', 'tm'), ('tile', 'arrow')), parts along dimension 0, may hold values from -3 to 3
- arrow_rhs: float32 [192, 64], P(('groups', 'tile', 'arrow')), parts along dimension 0, may hold values from -6 to 6
- diag_inverse: bfloat16 [8, 1024, 1024], P(('groups', 'tm'), None, ('tile', 'arrow')), parts along dimension 0
- lower_coupling: bfloat16 [8, 1024, 1024], P(('groups', 'tm'), None, ('tile', 'arrow')), parts along dimension 0
- arrow_slab: bfloat16 [8, 64, 1024], P(('groups', 'tm'), 'arrow'), parts along dimension 0, may hold values from -0.09375 to 0.09375
- arrow_inverse: float32 [128, 64], P('groups'), parts along dimension 0
- boundary_term: float32 [192, 1024], P(('groups', 'tile', 'arrow')), parts along dimension 0, may hold values from -6 to 6
Outputs:
- solution: float32 [8, 96, 1024], P(('groups', 'tm'), ('tile', 'arrow')), parts along dimension 0
- arrow_solution: float32 [192, 64], P(('groups', 'tile', 'arrow')), parts along dimension 0
There are 2 independent parts, one for each index of `groups`. A program takes and returns all parts, laid end to end along the dimension named above; each array names one. Nothing has to cross between parts.
All inputs are finite; a program needn't handle non-finite values.
Results may differ from a plain program's by a relative error of at most 0.007.
Values may be sent and summed in bfloat16 or wider, within the bound.
A program may use at most 64 MiB of HBM per device.

v0:
```python
import jax
import jax.numpy as jnp
from jax import lax
from jax.sharding import PartitionSpec as P


def from_behind(block, axis, distance):
    devices = range(lax.axis_size(axis))
    route = [(i - distance, i) for i in devices if i - distance in devices]
    return lax.ppermute(block, axis, route)


def shards(
    forward_blocks,
    arrow_rhs,
    diag_inverse,
    lower_coupling,
    arrow_slab,
    arrow_inverse,
    boundary_term,
):
    highest = lax.Precision.HIGHEST
    slab_full = lax.all_gather(arrow_slab, "arrow", axis=1, tiled=True)
    slab_wide = slab_full[0].astype(jnp.float32)
    block_rows = forward_blocks[0]
    local_part = jnp.dot(block_rows, slab_wide.T, precision=highest)
    arrow_sum = lax.psum(local_part, "tm")
    arrow_forward = jnp.dot(arrow_rhs - arrow_sum, arrow_inverse.T, precision=highest)
    arrow_solution = jnp.dot(arrow_forward, arrow_inverse, precision=highest)
    arrow_term = jnp.dot(arrow_solution, slab_wide, precision=highest)
    source_rows = block_rows - arrow_term
    inverse_full, lower_full = (
        lax.all_gather(diag_inverse, ("tile", "arrow"), axis=2, tiled=True),
        lax.all_gather(lower_coupling, ("tile", "arrow"), axis=2, tiled=True),
    )
    coupling = jnp.dot(inverse_full[0], lower_full[0], preferred_element_type=jnp.float32).astype(
        jnp.bfloat16
    )
    coupling_wide = coupling.astype(jnp.float32)
    is_last = (lax.axis_index("tm") == lax.axis_size("tm") - 1).astype(jnp.float32)
    entry_term = is_last * boundary_term

    def one_turn(turn_index, carry_in):
        residual = source_rows - carry_in
        outgoing = jnp.dot(residual, coupling_wide, precision=highest)
        return entry_term + from_behind(outgoing, "tm", -1)

    carry_in = lax.fori_loop(0, lax.axis_size("tm") - 1, one_turn, entry_term)
    residual = source_rows - carry_in
    solution = jnp.dot(
        residual.astype(jnp.bfloat16), inverse_full[0], preferred_element_type=jnp.float32
    )
    return (solution[None], arrow_solution)


def solution(mesh):
    return jax.shard_map(
        shards,
        mesh=mesh,
        in_specs=(
            P(("groups", "tm"), ("tile", "arrow"), None),
            P(("groups", "tile", "arrow"), None),
            P(("groups", "tm"), None, ("tile", "arrow")),
            P(("groups", "tm"), None, ("tile", "arrow")),
            P(("groups", "tm"), "arrow", None),
            P("groups", None),
            P(("groups", "tile", "arrow"), None),
        ),
        out_specs=(
            P(("groups", "tm"), ("tile", "arrow"), None),
            P(("groups", "tile", "arrow"), None),
        ),
        check_vma=False,
    )
```

profile of v0, /device:TPU:0, one launch (start us, length us, event | category | flops | bytes accessed | tf_op | source)
XLA Modules:
  0.0 106.9 jit_solution(2100586051761688842)
XLA Ops:
  7.2 0.0 copy-start
  7.2 0.0 copy-start.2
  7.2 0.0 all-gather.3.cloned.1.call-start
  7.2 0.7 all-gather.3.cloned.1.call-update
  7.9 0.0 all-gather.5.cloned.1.call-start
  8.0 0.7 all-gather.5.cloned.1.call-update
  8.7 0.9 broadcast_multiply_fusion
  9.6 2.2 %all_gather.9 = bf16[1,64,1024]{2,1,0:T(8,128)(2,1)S(1)} all-gather(bf16[1,32,1024]{2,1,0:T(8,128)(2,1)} %param.13), channel_id=1, replica_groups=mesh['groups'=2,'tm'=4,'tile'=2,'arrow'=2] {'arrow'}, dimensions={1}, use_global_device_ids=true | all-gather | bytes 196608 | tf_op jit(solution)/shard_map/all_gather | solution.py:23
  11.8 1.1 fusion.15
  12.9 20.3 %psum.7 = f32[24,64]{1,0:T(8,128)S(1)} all-reduce(f32[24,64]{1,0:T(8,128)S(1)} %fusion.15), channel_id=1, replica_groups=mesh['groups'=2,'tm'=4,'tile'=2,'arrow'=2] {'tm'}, use_global_device_ids=true, to_apply=%region_0.0 | all-reduce | flops 1536 | bytes 12288 | tf_op jit(solution)/shard_map/psum | solution.py:27
  33.2 0.0 copy-done
  33.2 0.9 fusion.18
  34.1 0.2 fusion.20
  34.2 0.0 copy-done.2
  34.3 0.0 copy-start.3
  34.3 0.2 convolution_subtract_fusion
  34.5 0.7 all-gather.3.cloned.1.call-done
  35.1 24.4 %all-gather.5.cloned.1.call-done = bf16[1,1024,1024]{2,1,0:T(8,128)(2,1)} async-done(((bf16[1,1024,256]{2,1,0:T(8,128)(2,1)}), bf16[1,1024,1024]{2,1,0:T(8,128)(2,1)}) %all-gather.5.cloned.1.call-update) | async-done | bytes 2097168 | tf_op jit(solution)/shard_map/all_gather | solution.py:34
  59.6 6.5 %convert_convert_fusion = f32[1024,1024]{1,0:T(8,128)} fusion(bf16[1,1024,1024]{2,1,0:T(8,128)(2,1)} %all-gather.5.cloned.1.call-done, bf16[1,1024,1024]{2,1,0:T(8,128)(2,1)} %all-gather.3.cloned.1.call-done), kind=kOutput, calls=%fused_computation.7 | convolution fusion | flops 2149580800 | bytes 8388608 | tf_op jit(solution)/shard_map/dot_general | solution.py:36
  66.1 0.0 copy-done.3
  66.1 32.9 %while.10 = (s32[]{:T(128)}, f32[24,1024]{1,0:T(8,128)S(1)}, f32[24,1024]{1,0:T(8,128)S(1)}, f32[1024,1024]{1,0:T(8,128)}, f32[24,1024]{1,0:T(8,128)S(1)}, /*index=5*/s32[]{:T(128)}) while((s32[]{:T(128)}, f32[24,1024]{1,0:T(8,128)S(1)}, f32[24,1024]{1,0:T(8,128)S(1)}, f32[1024,1024]{1,0:T(8,128)}, f32[24,1024]{1,0:T(8,128)S(1)}, ...), condition=%wide.region_2.0_spmd, body=%wide.region_1.0_spmd.sunk | while | flops 302039040 | bytes 5177453 | solution.py:48
  66.1 4.4 %fusion.31 = f32[24,1024]{1,0:T(8,128)S(1)} fusion(f32[1024,1024]{1,0:T(8,128)} %get-tuple-element.86, f32[24,1024]{1,0:T(8,128)S(1)} %get-tuple-element.85, f32[24,1024]{1,0:T(8,128)S(1)} %get-tuple-element.78), kind=kOutput, calls=%fused_computation.clone.1 | convolution fusion | flops 302014464 | bytes 4489216 | tf_op jit(solution)/shard_map/while/body/eval_jaxpr/dot_general | solution.py:45
  70.5 1.3 %collective-permute-start = (f32[24,1024]{1,0:T(8,128)S(1)}, f32[24,1024]{1,0:T(8,128)S(1)}, u32[]{:S(2)}, u32[]{:S(2)}) collective-permute-start(f32[24,1024]{1,0:T(8,128)S(1)} %fusion.31), channel_id=1, source_target_pairs={{4,0},{8,4},{12,8},{5,1},{9,5},{13,9},{6,2},{10,6},{14,10},{7,3},{... | collective-permute-start | bytes 294920 | tf_op jit(solution)/shard_map/while/body/eval_jaxpr/ppermute | solution.py:10
  71.8 5.6 %collective-permute-done = f32[24,1024]{1,0:T(8,128)S(1)} collective-permute-done((f32[24,1024]{1,0:T(8,128)S(1)}, f32[24,1024]{1,0:T(8,128)S(1)}, u32[]{:S(2)}, u32[]{:S(2)}) %collective-permute-start) | collective-permute-done | bytes 98336 | tf_op jit(solution)/shard_map/while/body/eval_jaxpr/ppermute | solution.py:10
  77.4 4.3 %fusion.31 = f32[24,1024]{1,0:T(8,128)S(1)} fusion(f32[1024,1024]{1,0:T(8,128)} %get-tuple-element.86, f32[24,1024]{1,0:T(8,128)S(1)} %get-tuple-element.85, f32[24,1024]{1,0:T(8,128)S(1)} %get-tuple-element.78), kind=kOutput, calls=%fused_computation.clone.1 | convolution fusion | flops 302014464 | bytes 4489216 | tf_op jit(solution)/shard_map/while/body/eval_jaxpr/dot_general | solution.py:45
  81.7 1.3 %collective-permute-start = (f32[24,1024]{1,0:T(8,128)S(1)}, f32[24,1024]{1,0:T(8,128)S(1)}, u32[]{:S(2)}, u32[]{:S(2)}) collective-permute-start(f32[24,1024]{1,0:T(8,128)S(1)} %fusion.31), channel_id=1, source_target_pairs={{4,0},{8,4},{12,8},{5,1},{9,5},{13,9},{6,2},{10,6},{14,10},{7,3},{... | collective-permute-start | bytes 294920 | tf_op jit(solution)/shard_map/while/body/eval_jaxpr/ppermute | solution.py:10
  83.0 5.2 %collective-permute-done = f32[24,1024]{1,0:T(8,128)S(1)} collective-permute-done((f32[24,1024]{1,0:T(8,128)S(1)}, f32[24,1024]{1,0:T(8,128)S(1)}, u32[]{:S(2)}, u32[]{:S(2)}) %collective-permute-start) | collective-permute-done | bytes 98336 | tf_op jit(solution)/shard_map/while/body/eval_jaxpr/ppermute | solution.py:10
  88.2 4.3 %fusion.31 = f32[24,1024]{1,0:T(8,128)S(1)} fusion(f32[1024,1024]{1,0:T(8,128)} %get-tuple-element.86, f32[24,1024]{1,0:T(8,128)S(1)} %get-tuple-element.85, f32[24,1024]{1,0:T(8,128)S(1)} %get-tuple-element.78), kind=kOutput, calls=%fused_computation.clone.1 | convolution fusion | flops 302014464 | bytes 4489216 | tf_op jit(solution)/shard_map/while/body/eval_jaxpr/dot_general | solution.py:45
  92.5 1.3 %collective-permute-start = (f32[24,1024]{1,0:T(8,128)S(1)}, f32[24,1024]{1,0:T(8,128)S(1)}, u32[]{:S(2)}, u32[]{:S(2)}) collective-permute-start(f32[24,1024]{1,0:T(8,128)S(1)} %fusion.31), channel_id=1, source_target_pairs={{4,0},{8,4},{12,8},{5,1},{9,5},{13,9},{6,2},{10,6},{14,10},{7,3},{... | collective-permute-start | bytes 294920 | tf_op jit(solution)/shard_map/while/body/eval_jaxpr/ppermute | solution.py:10
  93.8 5.2 %collective-permute-done = f32[24,1024]{1,0:T(8,128)S(1)} collective-permute-done((f32[24,1024]{1,0:T(8,128)S(1)}, f32[24,1024]{1,0:T(8,128)S(1)}, u32[]{:S(2)}, u32[]{:S(2)}) %collective-permute-start) | collective-permute-done | bytes 98336 | tf_op jit(solution)/shard_map/while/body/eval_jaxpr/ppermute | solution.py:10
  99.0 0.0 copy-done.1
  99.0 1.0 fusion.11
  (5 shorter events, 0.0 us)
Async XLA Ops:
  7.2 26.0 %copy-start = (f32[64,64]{1,0:T(8,128)S(1)}, f32[64,64]{1,0:T(8,128)}, u32[]{:S(2)}) copy-start(f32[64,64]{1,0:T(8,128)} %param.14) | copy-start | bytes 49156
  7.2 27.1 %copy-start.2 = (f32[1,24,1024]{2,1,0:T(8,128)S(1)}, f32[1,24,1024]{2,1,0:T(8,128)}, u32[]{:S(2)}) copy-start(f32[1,24,1024]{2,1,0:T(8,128)} %param.9) | copy-start | bytes 294916
  7.2 28.0 %all-gather.3.cloned.1.call-start = ((), (), s32[]{:S(2)}) async-start(), calls=%async_computation | async-start | bytes 2621440 | tf_op jit(solution)/shard_map/all_gather | solution.py:33
  7.9 51.6 %all-gather.5.cloned.1.call-start = ((), (), s32[]{:S(2)}) async-start(), calls=%async_computation.1 | async-start | bytes 2621440 | tf_op jit(solution)/shard_map/all_gather | solution.py:34
  34.3 31.8 %copy-start.3 = (f32[24,64]{1,0:T(8,128)}, f32[24,64]{1,0:T(8,128)S(1)}, u32[]{:S(2)}) copy-start(f32[24,64]{1,0:T(8,128)S(1)} %fusion.20) | copy-start | bytes 18436
  66.1 33.0 %copy-start.1 = (bf16[1,1024,1024]{2,1,0:T(8,128)(2,1)S(1)}, bf16[1,1024,1024]{2,1,0:T(8,128)(2,1)}, u32[]{:S(2)}) copy-start(bf16[1,1024,1024]{2,1,0:T(8,128)(2,1)} %all-gather.3.cloned.1.call-done) | copy-start | bytes 6291460
  70.5 6.8 %collective-permute-start = (f32[24,1024]{1,0:T(8,128)S(1)}, f32[24,1024]{1,0:T(8,128)S(1)}, u32[]{:S(2)}, u32[]{:S(2)}) collective-permute-start(f32[24,1024]{1,0:T(8,128)S(1)} %fusion.31), channel_id=1, source_target_pairs={{4,0},{8,4},{12,8},{5,1},{9,5},{13,9},{6,2},{10,6},{14,10},{7,3},{... | collective-permute-start | bytes 294920 | tf_op jit(solution)/shard_map/while/body/eval_jaxpr/ppermute | solution.py:10
  81.7 6.5 %collective-permute-start = (f32[24,1024]{1,0:T(8,128)S(1)}, f32[24,1024]{1,0:T(8,128)S(1)}, u32[]{:S(2)}, u32[]{:S(2)}) collective-permute-start(f32[24,1024]{1,0:T(8,128)S(1)} %fusion.31), channel_id=1, source_target_pairs={{4,0},{8,4},{12,8},{5,1},{9,5},{13,9},{6,2},{10,6},{14,10},{7,3},{... | collective-permute-start | bytes 294920 | tf_op jit(solution)/shard_map/while/body/eval_jaxpr/ppermute | solution.py:10
  92.5 6.5 %collective-permute-start = (f32[24,1024]{1,0:T(8,128)S(1)}, f32[24,1024]{1,0:T(8,128)S(1)}, u32[]{:S(2)}, u32[]{:S(2)}) collective-permute-start(f32[24,1024]{1,0:T(8,128)S(1)} %fusion.31), channel_id=1, source_target_pairs={{4,0},{8,4},{12,8},{5,1},{9,5},{13,9},{6,2},{10,6},{14,10},{7,3},{... | collective-permute-start | bytes 294920 | tf_op jit(solution)/shard_map/while/body/eval_jaxpr/ppermute | solution.py:10
Sparse Core Ops, SparseCore 0:
  9.6 25.5 all-gather.2
  36.7 22.8 all-gather.4
where the time goes:
time: 107 us
  waiting for transfers between devices  42.5 us (40%)
  matrix products  22.8 us (21%)
  blocking collectives  22.6 us (21%)
  between operations  14.1 us (13%)
  starting transfers between devices  3.94 us (4%)
    all_gather x1, waiting for transfers between devices, shards(): lax.all_gather(lower_coupling, ('tile', 'arrow'), axis=2, tiled=True)  24.4 us
    psum x1, blocking collectives, shards(): arrow_sum = lax.psum(local_part, 'tm')  20.3 us
    ppermute x3, waiting for transfers between devices, from_behind(): return lax.ppermute(block, axis, route)  16 us
    dot_general x3, matrix products, one_turn(): outgoing = jnp.dot(residual, coupling_wide, precision=highest)  13 us
    dot_general x1, matrix products, shards(): jnp.dot(inverse_full[0], lower_full[0], preferred_element_type=jnp.float32)  6.5 us
    ppermute x3, starting transfers between devices, from_behind(): return lax.ppermute(block, axis, route)  3.86 us
    all_gather x1, blocking collectives, shards(): slab_full = lax.all_gather(arrow_slab, 'arrow', axis=1, tiled=True)  2.21 us
  transfers between devices with their start and end apart: 5, of which 5 were waited for; matrix products, arithmetic and copies ran while one was open for 3% of the time, Pallas kernels for 0%

commit v1 on v0

--- a/solution.py
+++ b/solution.py
@@ -2,6 +2,19 @@
 import jax.numpy as jnp
 from jax import lax
 from jax.sharding import PartitionSpec as P
+
+
+def ring_gather(x, axis, dim):
+    ways = lax.axis_size(axis)
+    up = [(d, (d + 1) % ways) for d in range(ways)]
+    down = [(d, (d - 1) % ways) for d in range(ways)]
+    earlier, later = ([x], [x])
+    for _ in range(ways // 2):
+        earlier.append(lax.ppermute(earlier[-1], axis, up))
+    for _ in range((ways - 1) // 2):
+        later.append(lax.ppermute(later[-1], axis, down))
+    line = jnp.concatenate([*earlier[::-1], *later[1:]], axis=dim)
+    return jnp.roll(line, (lax.axis_index(axis) - ways // 2) * x.shape[dim], axis=dim)
 
 
 def from_behind(block, axis, distance):
@@ -31,7 +44,7 @@
     source_rows = block_rows - arrow_term
     inverse_full, lower_full = (
         lax.all_gather(diag_inverse, ("tile", "arrow"), axis=2, tiled=True),
-        lax.all_gather(lower_coupling, ("tile", "arrow"), axis=2, tiled=True),
+        ring_gather(lower_coupling, ("tile", "arrow"), 2),
     )
     coupling = jnp.dot(inverse_full[0], lower_full[0], preferred_element_type=jnp.float32).astype(
         jnp.bfloat16

time: 107 us -> 97.4 us (0.910)
  waiting for transfers between devices: 42.5 us -> 22.7 us
  local copies, waits for them, and re-layouts: 0.04 us -> 7.06 us
  starting transfers between devices: 3.94 us -> 6.45 us
    all_gather x1 -> x0, waiting for transfers between devices: 24.4 us -> none  [shards(): lax.all_gather(lower_coupling, ('tile', 'arrow'), axis=2, tiled=True)]
    ppermute x0 -> x3, waiting for transfers between devices: none -> 6.41 us  [the longest x2 6.41 us: ring_gather(): earlier.append(lax.ppermute(earlier[-1], axis, up))]
    unnamed x9 -> x16, local copies, waits for them, and re-layouts: 0.04 us -> 6.17 us
    ppermute x0 -> x3, starting transfers between devices: none -> 2.55 us  [the longest x1 1.99 us: ring_gather(): later.append(lax.ppermute(later[-1], axis, down))]
  transfers between devices with their start and end apart: 5 -> 7, of which waited for: 5 -> 4; matrix products, arithmetic and copies ran while one was open for 3% -> 11% of each run, Pallas kernels for 0% -> 0%
where the time goes in v1:
time: 97.4 us; the launch traced here: 96.9 us
  matrix products  23.7 us (24%)
  waiting for transfers between devices  22.7 us (23%)
  blocking collectives  21.8 us (22%)
  between operations  14.2 us (15%)
  local copies, waits for them, and re-layouts  7.06 us (7%)
  starting transfers between devices  6.45 us (7%)
    psum x1, blocking collectives, shards(): arrow_sum = lax.psum(local_part, 'tm')  19.5 us
    ppermute x3, waiting for transfers between devices, from_behind(): return lax.ppermute(block, axis, route)  15.6 us
    dot_general x3, matrix products, one_turn(): outgoing = jnp.dot(residual, coupling_wide, precision=highest)  13 us
    dot_general x1, matrix products, shards(): jnp.dot(inverse_full[0], lower_full[0], preferred_element_type=jnp.float32)  6.5 us
    ppermute x2, waiting for transfers between devices, ring_gather(): earlier.append(lax.ppermute(earlier[-1], axis, up))  6.41 us
    unnamed x16, local copies, waits for them, and re-layouts  6.17 us
    ppermute x3, starting transfers between devices, from_behind(): return lax.ppermute(block, axis, route)  3.86 us
    all_gather x1, blocking collectives, shards(): slab_full = lax.all_gather(arrow_slab, 'arrow', axis=1, tiled=True)  2.36 us
  transfers between devices with their start and end apart: 7, of which 4 were waited for; matrix products, arithmetic and copies ran while one was open for 11% of the time, Pallas kernels for 0%

profile of v1, /device:TPU:0, one launch (start us, length us, event | category | flops | bytes accessed | tf_op | source)
XLA Modules:
  0.0 96.9 jit_solution(5160209827441134845)
XLA Ops:
  7.2 0.7 all-gather.2.cloned.1.call-update
  7.9 0.5 collective-permute-start.1
  8.4 2.0 %collective-permute-start.3 = (bf16[1,1024,256]{2,1,0:T(8,128)(2,1)}, bf16[1,1024,256]{2,1,0:T(8,128)(2,1)S(1)}, u32[]{:S(2)}, u32[]{:S(2)}) collective-permute-start(bf16[1,1024,256]{2,1,0:T(8,128)(2,1)} %param.12), channel_id=1, source_target_pairs={{0,3},{1,0},{2,1},{3,2},{4,7},{5,4},{6,5},{7,6},{8,11},{9,8},{10,9... | collective-permute-start | bytes 1572872 | tf_op jit(solution)/shard_map/ppermute | solution.py:15
  10.4 2.4 %all_gather.6 = bf16[1,64,1024]{2,1,0:T(8,128)(2,1)S(1)} all-gather(bf16[1,32,1024]{2,1,0:T(8,128)(2,1)} %param.13), channel_id=1, replica_groups=mesh['groups'=2,'tm'=4,'tile'=2,'arrow'=2] {'arrow'}, dimensions={1}, use_global_device_ids=true | all-gather | bytes 196608 | tf_op jit(solution)/shard_map/all_gather | solution.py:36
  12.8 1.1 %fusion.16 = f32[24,64]{1,0:T(8,128)S(1)} fusion(bf16[1,64,1024]{2,1,0:T(8,128)(2,1)S(1)} %all_gather.6, f32[1,24,1024]{2,1,0:T(8,128)} %param.9), kind=kOutput, calls=%fused_computation.12 | convolution fusion | flops 18874368 | bytes 235520 | tf_op jit(solution)/shard_map/dot_general | solution.py:39
  13.8 19.5 %psum.7 = f32[24,64]{1,0:T(8,128)S(1)} all-reduce(f32[24,64]{1,0:T(8,128)S(1)} %fusion.16), channel_id=1, replica_groups=mesh['groups'=2,'tm'=4,'tile'=2,'arrow'=2] {'tm'}, use_global_device_ids=true, to_apply=%region_0.0 | all-reduce | flops 1536 | bytes 12288 | tf_op jit(solution)/shard_map/psum | solution.py:40
  33.3 0.9 broadcast_multiply_fusion
  34.2 0.1 collective-permute-start.2
  34.3 0.9 fusion.19
  35.2 0.1 fusion.22
  35.4 1.1 %convolution_subtract_fusion = f32[24,1024]{1,0:T(8,128)S(1)} fusion(f32[24,64]{1,0:T(8,128)S(1)} %fusion.22, bf16[1,64,1024]{2,1,0:T(8,128)(2,1)S(1)} %all_gather.6, f32[1,24,1024]{2,1,0:T(8,128)} %param.9), kind=kOutput, calls=%fused_computation.10 | convolution fusion | flops 18898944 | bytes 333824 | tf_op jit(solution)/shard_map/dot_general | solution.py:43
  36.5 6.4 %collective-permute-done.2 = bf16[1,1024,256]{2,1,0:T(8,128)(2,1)S(1)} collective-permute-done((bf16[1,1024,256]{2,1,0:T(8,128)(2,1)S(1)}, bf16[1,1024,256]{2,1,0:T(8,128)(2,1)S(1)}, u32[]{:S(2)}, u32[]{:S(2)}) %collective-permute-start.2) | collective-permute-done | bytes 524320 | tf_op jit(solution)/shard_map/ppermute | solution.py:13
  42.9 0.9 constant_dynamic-update-slice_fusion.7
  43.8 0.9 constant_dynamic-update-slice_fusion.6
  44.7 0.9 constant_dynamic-update-slice_fusion.5
  45.5 0.9 constant_dynamic-update-slice_fusion.4
  46.4 0.9 constant_dynamic-update-slice_fusion.3
  47.3 0.9 constant_dynamic-update-slice_fusion.2
  48.2 0.9 constant_dynamic-update-slice_fusion.1
  49.0 0.9 constant_dynamic-update-slice_fusion
  49.9 6.5 %convert_bitcast_fusion = f32[1024,1024]{1,0:T(8,128)} fusion(bf16[1,1024,2048]{2,1,0:T(8,128)(2,1)} %constant_dynamic-update-slice_fusion, s32[]{:T(128)S(6)} %select_n.14, bf16[1,1024,1024]{2,1,0:T(8,128)(2,1)} %all-gather.2.cloned.1.call-done), kind=kOutput, calls=%fused_computation.2 | convolution fusion | flops 2149580800 | bytes 8388612 | tf_op jit(solution)/shard_map/dot_general | solution.py:49
  56.4 32.6 %while.10 = (s32[]{:T(128)}, f32[24,1024]{1,0:T(8,128)S(1)}, f32[24,1024]{1,0:T(8,128)S(1)}, f32[1024,1024]{1,0:T(8,128)}, f32[24,1024]{1,0:T(8,128)S(1)}, /*index=5*/s32[]{:T(128)}) while((s32[]{:T(128)}, f32[24,1024]{1,0:T(8,128)S(1)}, f32[24,1024]{1,0:T(8,128)S(1)}, f32[1024,1024]{1,0:T(8,128)}, f32[24,1024]{1,0:T(8,128)S(1)}, ...), condition=%wide.region_2.3_spmd, body=%wide.region_1.2_spmd.sunk | while | flops 302039040 | bytes 5177453 | solution.py:61
  56.4 4.4 %fusion.33 = f32[24,1024]{1,0:T(8,128)S(1)} fusion(f32[1024,1024]{1,0:T(8,128)} %get-tuple-element.86, f32[24,1024]{1,0:T(8,128)S(1)} %get-tuple-element.85, f32[24,1024]{1,0:T(8,128)S(1)} %get-tuple-element.78), kind=kOutput, calls=%fused_computation.clone.1 | convolution fusion | flops 302014464 | bytes 4489216 | tf_op jit(solution)/shard_map/while/body/eval_jaxpr/dot_general | solution.py:58
  60.9 1.3 %collective-permute-start = (f32[24,1024]{1,0:T(8,128)S(1)}, f32[24,1024]{1,0:T(8,128)S(1)}, u32[]{:S(2)}, u32[]{:S(2)}) collective-permute-start(f32[24,1024]{1,0:T(8,128)S(1)} %fusion.33), channel_id=1, source_target_pairs={{4,0},{8,4},{12,8},{5,1},{9,5},{13,9},{6,2},{10,6},{14,10},{7,3},{... | collective-permute-start | bytes 294920 | tf_op jit(solution)/shard_map/while/body/eval_jaxpr/ppermute | solution.py:23
  62.2 5.2 %collective-permute-done = f32[24,1024]{1,0:T(8,128)S(1)} collective-permute-done((f32[24,1024]{1,0:T(8,128)S(1)}, f32[24,1024]{1,0:T(8,128)S(1)}, u32[]{:S(2)}, u32[]{:S(2)}) %collective-permute-start) | collective-permute-done | bytes 98336 | tf_op jit(solution)/shard_map/while/body/eval_jaxpr/ppermute | solution.py:23
  67.4 4.3 %fusion.33 = f32[24,1024]{1,0:T(8,128)S(1)} fusion(f32[1024,1024]{1,0:T(8,128)} %get-tuple-element.86, f32[24,1024]{1,0:T(8,128)S(1)} %get-tuple-element.85, f32[24,1024]{1,0:T(8,128)S(1)} %get-tuple-element.78), kind=kOutput, calls=%fused_computation.clone.1 | convolution fusion | flops 302014464 | bytes 4489216 | tf_op jit(solution)/shard_map/while/body/eval_jaxpr/dot_general | solution.py:58
  71.7 1.3 %collective-permute-start = (f32[24,1024]{1,0:T(8,128)S(1)}, f32[24,1024]{1,0:T(8,128)S(1)}, u32[]{:S(2)}, u32[]{:S(2)}) collective-permute-start(f32[24,1024]{1,0:T(8,128)S(1)} %fusion.33), channel_id=1, source_target_pairs={{4,0},{8,4},{12,8},{5,1},{9,5},{13,9},{6,2},{10,6},{14,10},{7,3},{... | collective-permute-start | bytes 294920 | tf_op jit(solution)/shard_map/while/body/eval_jaxpr/ppermute | solution.py:23
  73.0 5.2 %collective-permute-done = f32[24,1024]{1,0:T(8,128)S(1)} collective-permute-done((f32[24,1024]{1,0:T(8,128)S(1)}, f32[24,1024]{1,0:T(8,128)S(1)}, u32[]{:S(2)}, u32[]{:S(2)}) %collective-permute-start) | collective-permute-done | bytes 98336 | tf_op jit(solution)/shard_map/while/body/eval_jaxpr/ppermute | solution.py:23
  78.2 4.3 %fusion.33 = f32[24,1024]{1,0:T(8,128)S(1)} fusion(f32[1024,1024]{1,0:T(8,128)} %get-tuple-element.86, f32[24,1024]{1,0:T(8,128)S(1)} %get-tuple-element.85, f32[24,1024]{1,0:T(8,128)S(1)} %get-tuple-element.78), kind=kOutput, calls=%fused_computation.clone.1 | convolution fusion | flops 302014464 | bytes 4489216 | tf_op jit(solution)/shard_map/while/body/eval_jaxpr/dot_general | solution.py:58
  82.5 1.3 %collective-permute-start = (f32[24,1024]{1,0:T(8,128)S(1)}, f32[24,1024]{1,0:T(8,128)S(1)}, u32[]{:S(2)}, u32[]{:S(2)}) collective-permute-start(f32[24,1024]{1,0:T(8,128)S(1)} %fusion.33), channel_id=1, source_target_pairs={{4,0},{8,4},{12,8},{5,1},{9,5},{13,9},{6,2},{10,6},{14,10},{7,3},{... | collective-permute-start | bytes 294920 | tf_op jit(solution)/shard_map/while/body/eval_jaxpr/ppermute | solution.py:23
  83.8 5.2 %collective-permute-done = f32[24,1024]{1,0:T(8,128)S(1)} collective-permute-done((f32[24,1024]{1,0:T(8,128)S(1)}, f32[24,1024]{1,0:T(8,128)S(1)}, u32[]{:S(2)}, u32[]{:S(2)}) %collective-permute-start) | collective-permute-done | bytes 98336 | tf_op jit(solution)/shard_map/while/body/eval_jaxpr/ppermute | solution.py:23
  89.1 1.0 %fusion.12 = f32[1,24,1024]{2,1,0:T(8,128)} fusion(bf16[1,1024,1024]{2,1,0:T(8,128)(2,1)S(1)} %copy-done.1, f32[24,1024]{1,0:T(8,128)S(1)} %get-tuple-element.90, f32[24,1024]{1,0:T(8,128)S(1)} %get-tuple-element.29), kind=kOutput, calls=%fused_computation.9 | convolution fusion | flops 50380800 | bytes 2392064 | tf_op jit(solution)/shard_map/dot_general | solution.py:63
  (16 shorter events, 0.1 us)
Async XLA Ops:
  7.2 27.1 %copy-start = (f32[64,64]{1,0:T(8,128)S(1)}, f32[64,64]{1,0:T(8,128)}, u32[]{:S(2)}) copy-start(f32[64,64]{1,0:T(8,128)} %param.14) | copy-start | bytes 49156
  7.2 37.5 %copy-start.2 = (bf16[1,1024,256]{2,1,0:T(8,128)(2,1)S(1)}, bf16[1,1024,256]{2,1,0:T(8,128)(2,1)}, u32[]{:S(2)}) copy-start(bf16[1,1024,256]{2,1,0:T(8,128)(2,1)} %param.12) | copy-start | bytes 1572868
  7.2 42.7 %all-gather.2.cloned.1.call-start = ((), (), s32[]{:S(2)}) async-start(), calls=%async_computation | async-start | bytes 2621440 | tf_op jit(solution)/shard_map/all_gather | solution.py:46
  7.9 26.3 %collective-permute-start.1 = (bf16[1,1024,256]{2,1,0:T(8,128)(2,1)}, bf16[1,1024,256]{2,1,0:T(8,128)(2,1)S(1)}, u32[]{:S(2)}, u32[]{:S(2)}) collective-permute-start(bf16[1,1024,256]{2,1,0:T(8,128)(2,1)} %param.12), channel_id=1, source_target_pairs={{0,1},{1,2},{2,3},{3,0},{4,5},{5,6},{6,7},{7,4},{8,9},{9,10},{10,1... | collective-permute-start | bytes 1572872 | tf_op jit(solution)/shard_map/ppermute | solution.py:13
  8.4 37.1 %collective-permute-start.3 = (bf16[1,1024,256]{2,1,0:T(8,128)(2,1)}, bf16[1,1024,256]{2,1,0:T(8,128)(2,1)S(1)}, u32[]{:S(2)}, u32[]{:S(2)}) collective-permute-start(bf16[1,1024,256]{2,1,0:T(8,128)(2,1)} %param.12), channel_id=1, source_target_pairs={{0,3},{1,0},{2,1},{3,2},{4,7},{5,4},{6,5},{7,6},{8,11},{9,8},{10,9... | collective-permute-start | bytes 1572872 | tf_op jit(solution)/shard_map/ppermute | solution.py:15
  34.2 8.7 %collective-permute-start.2 = (bf16[1,1024,256]{2,1,0:T(8,128)(2,1)S(1)}, bf16[1,1024,256]{2,1,0:T(8,128)(2,1)S(1)}, u32[]{:S(2)}, u32[]{:S(2)}) collective-permute-start(bf16[1,1024,256]{2,1,0:T(8,128)(2,1)S(1)} %collective-permute-done.1), channel_id=1, source_target_pairs={{0,1},{1,2},{2,3},{3,0},{4,5},{5,6},{6,7},{7,4},{8,9},{9,10},{10,1... | collective-permute-start | bytes 1572872 | tf_op jit(solution)/shard_map/ppermute | solution.py:13
  35.4 14.5 %copy-start.3 = (f32[24,64]{1,0:T(8,128)}, f32[24,64]{1,0:T(8,128)S(1)}, u32[]{:S(2)}) copy-start(f32[24,64]{1,0:T(8,128)S(1)} %fusion.22) | copy-start | bytes 18436
  56.4 32.6 %copy-start.1 = (bf16[1,1024,1024]{2,1,0:T(8,128)(2,1)S(1)}, bf16[1,1024,1024]{2,1,0:T(8,128)(2,1)}, u32[]{:S(2)}) copy-start(bf16[1,1024,1024]{2,1,0:T(8,128)(2,1)} %all-gather.2.cloned.1.call-done) | copy-start | bytes 6291460
  60.9 6.5 %collective-permute-start = (f32[24,1024]{1,0:T(8,128)S(1)}, f32[24,1024]{1,0:T(8,128)S(1)}, u32[]{:S(2)}, u32[]{:S(2)}) collective-permute-start(f32[24,1024]{1,0:T(8,128)S(1)} %fusion.33), channel_id=1, source_target_pairs={{4,0},{8,4},{12,8},{5,1},{9,5},{13,9},{6,2},{10,6},{14,10},{7,3},{... | collective-permute-start | bytes 294920 | tf_op jit(solution)/shard_map/while/body/eval_jaxpr/ppermute | solution.py:23
  71.7 6.5 %collective-permute-start = (f32[24,1024]{1,0:T(8,128)S(1)}, f32[24,1024]{1,0:T(8,128)S(1)}, u32[]{:S(2)}, u32[]{:S(2)}) collective-permute-start(f32[24,1024]{1,0:T(8,128)S(1)} %fusion.33), channel_id=1, source_target_pairs={{4,0},{8,4},{12,8},{5,1},{9,5},{13,9},{6,2},{10,6},{14,10},{7,3},{... | collective-permute-start | bytes 294920 | tf_op jit(solution)/shard_map/while/body/eval_jaxpr/ppermute | solution.py:23
  82.5 6.5 %collective-permute-start = (f32[24,1024]{1,0:T(8,128)S(1)}, f32[24,1024]{1,0:T(8,128)S(1)}, u32[]{:S(2)}, u32[]{:S(2)}) collective-permute-start(f32[24,1024]{1,0:T(8,128)S(1)} %fusion.33), channel_id=1, source_target_pairs={{4,0},{8,4},{12,8},{5,1},{9,5},{13,9},{6,2},{10,6},{14,10},{7,3},{... | collective-permute-start | bytes 294920 | tf_op jit(solution)/shard_map/while/body/eval_jaxpr/ppermute | solution.py:23
Sparse Core Ops, SparseCore 0:
  9.6 26.8 all-gather.1
